TPU v7x, 32 devices: a whole 2x2x4 slice. The times are simulated.
32 devices in a mesh: groups: 2 (over y), dp: 16 (over z, x, core).
Axes of the slice: x: 2, y: 2, z: 4, core: 2. Of those that a mesh axis runs over, the one named last changes fastest.
Arguments:
- activations: bfloat16 [4096, 14336], P(('groups', 'dp')), parts along dimension 0, may hold values from -6 to 6
- gradients: bfloat16 [4096, 8192], P(('groups', 'dp')), parts along dimension 0, may hold values from -6 to 6
- proj_in: bfloat16 [64, 14336], replicated, may hold values from -0.046875 to 0.046875
- proj_out: bfloat16 [64, 8192], replicated, may hold values from -0.0625 to 0.0625
- targets: bfloat16 [128, 4096], P(('groups', 'dp')), parts along dimension 0, may hold values from -6 to 6
- token_samples: int32 [4096], P(('groups', 'dp')), parts along dimension 0, may hold values from 0 to 31, as said below
- sample_rows: int32 [64], P('groups'), parts along dimension 0, may hold values from 0 to 31, each once
Outputs:
- scores: float32 [64, 64], P(('groups', 'dp')), parts along dimension 0
There are 2 independent parts, one for each index of `groups`. A program takes and returns all parts, laid end to end along the dimension named above; an argument that names none is the same for every part. Nothing has to cross between parts.
Inputs may be any that keep to these rules, and one draw needn't show every extreme that they name: `token_samples`: sample ids never fall along the 2048 tokens; each sample holds 48 to 80 consecutive tokens, both lengths occur, and the first two samples hold 64 tokens each.
All inputs are finite; a program needn't handle non-finite values.
Results may differ from a plain program's by a relative error of at most 0.0033.
Values may be sent and summed in bfloat16 or wider, within the bound.
A program may use at most 64 MiB of HBM per device.

v0:
```python
import jax
import jax.numpy as jnp
from jax import lax
from jax.sharding import PartitionSpec as P

LOCAL = 4


def partner(value, axis, bit):
    mask = 2**bit
    pairs = [(source, source ^ mask) for source in range(lax.axis_size(axis))]
    return lax.ppermute(value, axis, pairs)


def bit_value(own_index, position):
    return own_index >> position & 1


def split_half(values, axis, own_bit):
    shape = values.shape
    paired = values.reshape(shape[:axis] + (shape[axis] // 2, 2) + shape[axis + 1 :])
    kept_part = lax.dynamic_index_in_dim(paired, own_bit, axis + 1, keepdims=False)
    sent_part = lax.dynamic_index_in_dim(paired, 1 - own_bit, axis + 1, keepdims=False)
    return (kept_part, sent_part)


def joined_pair(kept_part, arrived, axis, own_bit):
    lower_first = jnp.concatenate([kept_part, arrived], axis=axis)
    upper_first = jnp.concatenate([arrived, kept_part], axis=axis)
    return jnp.where(own_bit == 0, lower_first, upper_first)


def on_device(activations, gradients, proj_in, proj_out, targets, token_samples, sample_rows):
    rank_size = proj_in.shape[0]
    square = rank_size * rank_size
    tokens_here = activations.shape[0]
    devices = lax.axis_size("dp")
    samples = sample_rows.shape[0]
    per_owner = samples // devices
    width = square // devices
    contract = (((1,), (1,)), ((), ()))
    in_factors = lax.dot_general(
        activations, proj_in, contract, preferred_element_type=jnp.float32
    ).astype(jnp.bfloat16)
    out_factors = lax.dot_general(
        gradients, proj_out, contract, preferred_element_type=jnp.float32
    ).astype(jnp.bfloat16)
    first_id = token_samples[0]
    last_id = token_samples[-1]
    columns = jnp.arange(LOCAL, dtype=jnp.int32)
    onehot = ((token_samples - first_id)[:, None] == columns[None, :]).astype(jnp.bfloat16)
    spread = (onehot[:, :, None] * out_factors[:, None, :]).reshape(tokens_here, LOCAL * rank_size)
    partials = lax.dot_general(
        spread, in_factors, (((0,), (0,)), ((), ())), preferred_element_type=jnp.float32
    )
    partials = partials.reshape(LOCAL, square)
    sample_ids = first_id + columns
    present = sample_ids <= last_id
    tags = jnp.where(present, sample_ids, samples)
    tag_table = jnp.broadcast_to(tags[:, None], (LOCAL, devices))
    received, received_ids = (
        lax.all_to_all(
            partials.reshape(LOCAL, devices, width), "dp", split_axis=1, concat_axis=0, tiled=True
        ),
        lax.all_to_all(tag_table, "dp", split_axis=1, concat_axis=0, tiled=True),
    )
    block = jax.ops.segment_sum(
        received.reshape(devices * LOCAL, width),
        received_ids.reshape(devices * LOCAL),
        num_segments=samples + 1,
    )[:samples]
    total = lax.psum(jnp.sum(block * block, axis=1), "dp")
    scale = lax.rsqrt(total / square + 1e-06)
    unit_block = (block * scale[:, None]).astype(jnp.bfloat16)
    placed_block = jnp.zeros((samples, width), jnp.bfloat16).at[sample_rows].set(unit_block)
    total_bits = devices.bit_length() - 1
    side_bits = total_bits // 3
    sum_bits = total_bits - 2 * side_bits
    side_count = 2**side_bits
    sum_count = 2**sum_bits
    own_index = lax.axis_index("dp")
    sketch_piece = placed_block.reshape(side_count, samples // side_count, width)
    for section in range(side_bits):
        position = sum_bits + side_bits + section
        own_bit = bit_value(own_index, position)
        kept_part, sent_part = split_half(sketch_piece, 0, own_bit)
        arrived = partner(sent_part, "dp", position)
        sketch_piece = joined_pair(kept_part, arrived, 2, own_bit)
    sketch_piece = sketch_piece.reshape(samples // side_count, -1)
    for section in range(side_bits):
        position = sum_bits + section
        own_bit = bit_value(own_index, position)
        arrived = partner(sketch_piece, "dp", position)
        sketch_piece = joined_pair(sketch_piece, arrived, 1, own_bit)
    target_count = targets.shape[0]
    target_piece = targets.reshape(target_count, side_count, side_count, sum_count, width)
    target_piece = jnp.transpose(target_piece, (0, 3, 2, 1, 4)).reshape(target_count, sum_count, -1)
    for section in range(sum_bits):
        position = section
        own_bit = bit_value(own_index, position)
        kept_part, sent_part = split_half(target_piece, 1, own_bit)
        arrived = partner(sent_part, "dp", position)
        target_piece = joined_pair(kept_part, arrived, 0, own_bit)
    target_piece = target_piece.reshape(target_piece.shape[0], -1)
    for section in range(side_bits):
        position = sum_bits + side_bits + section
        own_bit = bit_value(own_index, position)
        arrived = partner(target_piece, "dp", position)
        target_piece = joined_pair(target_piece, arrived, 0, own_bit)
    partial_value = (
        lax.dot_general(sketch_piece, target_piece, contract, preferred_element_type=jnp.float32)
        / rank_size
    )
    partial_value = partial_value.reshape(side_count, sum_count * per_owner, partial_value.shape[1])
    for section in range(side_bits):
        position = sum_bits + section
        own_bit = bit_value(own_index, position)
        kept_part, sent_part = split_half(partial_value, 0, own_bit)
        arrived = partner(sent_part, "dp", position)
        partial_value = joined_pair(kept_part, arrived, 2, own_bit)
    partial_value = partial_value.reshape(sum_count, per_owner, partial_value.shape[2])
    for section in range(sum_bits):
        position = section
        own_bit = bit_value(own_index, position)
        kept_part, sent_part = split_half(partial_value, 0, own_bit)
        arrived = partner(sent_part, "dp", position)
        partial_value = kept_part + arrived
    ordered = partial_value.reshape(per_owner, side_count, side_count, sum_count, target_count)
    scores = jnp.transpose(ordered, (0, 2, 1, 3, 4)).reshape(per_owner, -1)
    return scores


def solution(mesh):
    in_specs = (
        P(("groups", "dp"), None),
        P(("groups", "dp"), None),
        P(),
        P(),
        P(("groups", "dp"), None),
        P(("groups", "dp")),
        P("groups"),
    )
    out_specs = P(("groups", "dp"), None)
    return jax.shard_map(
        on_device, mesh=mesh, in_specs=in_specs, out_specs=out_specs, check_vma=False
    )
```

profile of v0, /device:TPU:0, one launch (start us, length us, event | category | flops | bytes accessed | tf_op | source)
XLA Modules:
  0.0 82.8 jit_solution(8969258779199845546)
XLA Ops:
  0.0 0.9 %reshape.135 = bf16[4,2,2,4,256]{4,3,2,1,0:T(4,128)(2,1)S(1)} reshape(bf16[4,4096]{1,0:T(4,128)(2,1)} %param.11) | data formatting | bytes 65536 | tf_op jit(solution)/shard_map/reshape | solution.py:96
  1.0 0.1 constant_dynamic-slice_fusion.8
  1.1 0.5 collective-permute-start.2
  1.6 1.3 %fusion.25 = (s32[1]{0:T(128)}, s32[1]{0:T(128)}) fusion(s32[128]{0:T(128)} %param.12), kind=kLoop, calls=%fused_computation.62 | loop fusion | bytes 16 | tf_op jit(solution)/shard_map/slice | solution.py:48
  2.9 1.2 %compare_select_fusion = s32[4]{0:T(128)S(1)} fusion(s32[]{:T(128)} %bitcast.1, s32[]{:T(128)} %bitcast), kind=kLoop, calls=%fused_computation.51 | loop fusion | flops 12 | bytes 24 | tf_op jit(solution)/shard_map/jit(_where)/select_n | solution.py:59
  4.2 0.6 broadcast_in_dim.28
  4.8 7.0 %all-to-all-start = ((s32[4,16,1]{0,2,1:T(1,128)}), s32[4,16,1]{0,2,1:T(1,128)S(1)}, u32[]{:S(2)}, u32[]{:S(2)}) async-start(s32[4,16,1]{0,2,1:T(1,128)} %broadcast_in_dim.28), calls=%async_computation | async-start | bytes 16384 | tf_op jit(solution)/shard_map/all_to_all | solution.py:65
  11.8 1.3 %broadcast_subtract_fusion = s32[128]{0:T(128)S(1)} fusion(s32[128]{0:T(128)} %param.12, s32[]{:T(128)} %bitcast), kind=kLoop, calls=%fused_computation.60 | loop fusion | flops 128 | bytes 1028 | tf_op jit(solution)/shard_map/sub | solution.py:51
  13.1 2.1 %convolution_convert_fusion.1 = bf16[128,64]{0,1:T(8,128)(2,1)S(1)} fusion(bf16[128,8192]{1,0:T(8,128)(2,1)S(1)} %copy-done, bf16[64,8192]{1,0:T(8,128)(2,1)} %param.10), kind=kOutput, calls=%fused_computation.3 | convolution fusion | flops 134225920 | bytes 3162112 | tf_op jit(solution)/shard_map/dot_general | solution.py:45
  15.2 4.2 %fusion = f32[256,64]{1,0:T(8,128)S(1)} fusion(bf16[128,256]{0,1:T(8,128)(2,1)S(1)} %bitcast.49, bf16[128,14336]{1,0:T(8,128)(2,1)} %param.7, bf16[64,14336]{1,0:T(8,128)(2,1)} %param.9), kind=kOutput, calls=%fused_computation.4 | convolution fusion | flops 239083520 | bytes 5636096 | tf_op jit(solution)/shard_map/dot_general | solution.py:53
  19.5 0.1 reshape_reshape.13
  19.6 0.7 copy.22
  20.3 6.0 %all-to-all-start.1 = ((f32[4,16,256]{2,0,1:T(4,128)}), f32[4,16,256]{2,0,1:T(4,128)S(1)}, u32[]{:S(2)}, u32[]{:S(2)}) async-start(f32[4,16,256]{2,0,1:T(4,128)} %copy.22), calls=%async_computation.1 | async-start | bytes 131072 | tf_op jit(solution)/shard_map/all_to_all | solution.py:62
  26.3 0.1 constant_dynamic-slice_fusion.6
  26.4 2.0 %collective-permute-start.3 = (bf16[8,1,1024]{2,1,0:T(2,128)(2,1)S(1)}, bf16[8,1,1024]{2,1,0:T(2,128)(2,1)S(1)}, u32[]{:S(2)}, u32[]{:S(2)}) collective-permute-start(bf16[8,1,1024]{2,1,0:T(2,128)(2,1)S(1)} %get-tuple-element.6), channel_id=1, source_target_pairs={{0,2},{1,3},{2,0},{3,1},{4,6},{5,7},{6,4},{7,5},{8,10},{9,11},{10,... | collective-permute-start | bytes 49160 | tf_op jit(solution)/shard_map/ppermute | solution.py:12
  28.4 0.1 reshape.140
  28.5 1.9 %collective-permute-done.3 = bf16[8,1,1024]{2,1,0:T(2,128)(2,1)S(1)} collective-permute-done((bf16[8,1,1024]{2,1,0:T(2,128)(2,1)S(1)}, bf16[8,1,1024]{2,1,0:T(2,128)(2,1)S(1)}, u32[]{:S(2)}, u32[]{:S(2)}) %collective-permute-start.3) | collective-permute-done | bytes 16416 | tf_op jit(solution)/shard_map/ppermute | solution.py:12
  30.4 2.8 %all-to-all-done.1 = f32[4,16,256]{2,0,1:T(4,128)S(1)} async-done(((f32[4,16,256]{2,0,1:T(4,128)}), f32[4,16,256]{2,0,1:T(4,128)S(1)}, u32[]{:S(2)}, u32[]{:S(2)}) %all-to-all-start.1) | async-done | bytes 65568 | tf_op jit(solution)/shard_map/all_to_all | solution.py:62
  33.2 0.9 %scatter_custom_fusion = f32[33,256]{1,0:T(8,128)S(1)} fusion(s32[64]{0:T(128)S(1)} %reshape.140, f32[64,256]{1,0:T(8,128)S(1)} %reshape.142, f32[]{:T(128)} %constant.65.clone.1), kind=kCustom, calls=%fused_computation.27 | custom fusion | flops 16384 | bytes 33796 | tf_op jit(solution)/shard_map/scatter-add | solution.py:67
  34.2 0.1 multiply_reduce_fusion
  34.3 29.9 %psum.7 = f32[32]{0:T(128)S(1)} all-reduce(f32[32]{0:T(128)S(1)} %multiply_reduce_fusion), channel_id=1, replica_groups=mesh['groups'=2,'dp'=16] {'dp'}, use_global_device_ids=true, to_apply=%region_2.3 | all-reduce | flops 32 | bytes 256 | tf_op jit(solution)/shard_map/psum | solution.py:72
  64.2 0.8 scatter_custom_fusion.1
  65.1 3.0 %collective-permute-start.4 = (bf16[16,1024]{1,0:T(8,128)(2,1)S(1)}, bf16[16,1024]{1,0:T(8,128)(2,1)S(1)}, u32[]{:S(2)}, u32[]{:S(2)}) collective-permute-start(bf16[16,1024]{1,0:T(8,128)(2,1)S(1)} %maximum_select_fusion.4), channel_id=1, source_target_pairs={{0,8},{1,9},{2,10},{3,11},{4,12},{5,13},{6,14},{7,15},{8,0},{9,1},... | collective-permute-start | bytes 98312 | tf_op jit(solution)/shard_map/ppermute | solution.py:12
  68.1 1.5 %collective-permute-done = bf16[1,16,256]{2,1,0:T(8,128)(2,1)S(1)} collective-permute-done((bf16[1,16,256]{2,1,0:T(8,128)(2,1)S(1)}, bf16[1,16,256]{2,1,0:T(8,128)(2,1)S(1)}, u32[]{:S(2)}, u32[]{:S(2)}) %collective-permute-start) | collective-permute-done | bytes 8224 | tf_op jit(solution)/shard_map/ppermute | solution.py:12
  69.7 0.3 collective-permute-done.4
  70.0 3.4 %collective-permute-done.1 = bf16[16,512]{1,0:T(8,128)(2,1)S(1)} collective-permute-done((bf16[16,512]{1,0:T(8,128)(2,1)S(1)}, bf16[16,512]{1,0:T(8,128)(2,1)S(1)}, u32[]{:S(2)}, u32[]{:S(2)}) %collective-permute-start.1) | collective-permute-done | bytes 16416 | tf_op jit(solution)/shard_map/ppermute | solution.py:12
  73.4 0.1 fusion.1
  73.6 3.6 %collective-permute-done.5 = f32[1,8,32]{2,1,0:T(8,128)S(1)} collective-permute-done((f32[1,8,32]{2,1,0:T(8,128)S(1)}, f32[1,8,32]{2,1,0:T(8,128)S(1)}, u32[]{:S(2)}, u32[]{:S(2)}) %collective-permute-start.5) | collective-permute-done | bytes 1056 | tf_op jit(solution)/shard_map/ppermute | solution.py:12
  77.3 1.1 %collective-permute-done.6 = f32[2,2,64]{2,1,0:T(2,128)S(1)} collective-permute-done((f32[2,2,64]{2,1,0:T(2,128)S(1)}, f32[2,2,64]{2,1,0:T(2,128)S(1)}, u32[]{:S(2)}, u32[]{:S(2)}) %collective-permute-start.6) | collective-permute-done | bytes 1056 | tf_op jit(solution)/shard_map/ppermute | solution.py:12
  78.5 3.6 %collective-permute-done.7 = f32[1,2,64]{2,1,0:T(2,128)S(1)} collective-permute-done((f32[1,2,64]{2,1,0:T(2,128)S(1)}, f32[1,2,64]{2,1,0:T(2,128)S(1)}, u32[]{:S(2)}, u32[]{:S(2)}) %collective-permute-start.7) | collective-permute-done | bytes 544 | tf_op jit(solution)/shard_map/ppermute | solution.py:12
  82.0 0.1 reshape.136
  82.2 0.7 reshape.137
  (34 shorter events, 0.5 us)
Async XLA Ops:
  0.0 13.1 %copy-start = (bf16[128,8192]{1,0:T(8,128)(2,1)S(1)}, bf16[128,8192]{1,0:T(8,128)(2,1)}, u32[]{:S(2)}) copy-start(bf16[128,8192]{1,0:T(8,128)(2,1)} %param.8) | copy-start | bytes 6291460
  1.1 19.1 %collective-permute-start.2 = (bf16[4,2,1024]{2,1,0:T(2,128)(2,1)S(1)}, bf16[4,2,1024]{2,1,0:T(2,128)(2,1)S(1)}, u32[]{:S(2)}, u32[]{:S(2)}) collective-permute-start(bf16[4,2,1024]{2,1,0:T(2,128)(2,1)S(1)} %bitcast.57), channel_id=1, source_target_pairs={{0,1},{1,0},{2,3},{3,2},{4,5},{5,4},{6,7},{7,6},{8,9},{9,8},{10,11... | collective-permute-start | bytes 49160 | tf_op jit(solution)/shard_map/ppermute | solution.py:12
  4.8 15.5 %all-to-all-start = ((s32[4,16,1]{0,2,1:T(1,128)}), s32[4,16,1]{0,2,1:T(1,128)S(1)}, u32[]{:S(2)}, u32[]{:S(2)}) async-start(s32[4,16,1]{0,2,1:T(1,128)} %broadcast_in_dim.28), calls=%async_computation | async-start | bytes 16384 | tf_op jit(solution)/shard_map/all_to_all | solution.py:65
  15.2 4.2 %copy-start.1 = (s32[32]{0:T(128)S(1)}, s32[32]{0:T(128)}, u32[]{:S(2)}) copy-start(s32[32]{0:T(128)} %param.13) | copy-start | bytes 388
  20.3 12.9 %all-to-all-start.1 = ((f32[4,16,256]{2,0,1:T(4,128)}), f32[4,16,256]{2,0,1:T(4,128)S(1)}, u32[]{:S(2)}, u32[]{:S(2)}) async-start(f32[4,16,256]{2,0,1:T(4,128)} %copy.22), calls=%async_computation.1 | async-start | bytes 131072 | tf_op jit(solution)/shard_map/all_to_all | solution.py:62
  26.4 4.0 %collective-permute-start.3 = (bf16[8,1,1024]{2,1,0:T(2,128)(2,1)S(1)}, bf16[8,1,1024]{2,1,0:T(2,128)(2,1)S(1)}, u32[]{:S(2)}, u32[]{:S(2)}) collective-permute-start(bf16[8,1,1024]{2,1,0:T(2,128)(2,1)S(1)} %get-tuple-element.6), channel_id=1, source_target_pairs={{0,2},{1,3},{2,0},{3,1},{4,6},{5,7},{6,4},{7,5},{8,10},{9,11},{10,... | collective-permute-start | bytes 49160 | tf_op jit(solution)/shard_map/ppermute | solution.py:12
  65.0 4.6 %collective-permute-start = (bf16[1,16,256]{2,1,0:T(8,128)(2,1)S(1)}, bf16[1,16,256]{2,1,0:T(8,128)(2,1)S(1)}, u32[]{:S(2)}, u32[]{:S(2)}) collective-permute-start(bf16[1,16,256]{2,1,0:T(8,128)(2,1)S(1)} %get-tuple-element.10), channel_id=1, source_target_pairs={{0,8},{1,9},{2,10},{3,11},{4,12},{5,13},{6,14},{7,15},{8,0},{9,1},... | collective-permute-start | bytes 24584 | tf_op jit(solution)/shard_map/ppermute | solution.py:12
  65.1 4.9 %collective-permute-start.4 = (bf16[16,1024]{1,0:T(8,128)(2,1)S(1)}, bf16[16,1024]{1,0:T(8,128)(2,1)S(1)}, u32[]{:S(2)}, u32[]{:S(2)}) collective-permute-start(bf16[16,1024]{1,0:T(8,128)(2,1)S(1)} %maximum_select_fusion.4), channel_id=1, source_target_pairs={{0,8},{1,9},{2,10},{3,11},{4,12},{5,13},{6,14},{7,15},{8,0},{9,1},... | collective-permute-start | bytes 98312 | tf_op jit(solution)/shard_map/ppermute | solution.py:12
  69.6 3.8 %collective-permute-start.1 = (bf16[16,512]{1,0:T(8,128)(2,1)S(1)}, bf16[16,512]{1,0:T(8,128)(2,1)S(1)}, u32[]{:S(2)}, u32[]{:S(2)}) collective-permute-start(bf16[16,512]{1,0:T(8,128)(2,1)S(1)} %maximum_select_fusion.5), channel_id=1, source_target_pairs={{0,4},{1,5},{2,6},{3,7},{4,0},{5,1},{6,2},{7,3},{8,12},{9,13},{10,... | collective-permute-start | bytes 49160 | tf_op jit(solution)/shard_map/ppermute | solution.py:12
  73.6 3.6 %collective-permute-start.5 = (f32[1,8,32]{2,1,0:T(8,128)S(1)}, f32[1,8,32]{2,1,0:T(8,128)S(1)}, u32[]{:S(2)}, u32[]{:S(2)}) collective-permute-start(f32[1,8,32]{2,1,0:T(8,128)S(1)} %get-tuple-element.12), channel_id=1, source_target_pairs={{0,4},{1,5},{2,6},{3,7},{4,0},{5,1},{6,2},{7,3},{8,12},{9,13},{10,... | collective-permute-start | bytes 3080 | tf_op jit(solution)/shard_map/ppermute | solution.py:12
  77.3 1.2 %collective-permute-start.6 = (f32[2,2,64]{2,1,0:T(2,128)S(1)}, f32[2,2,64]{2,1,0:T(2,128)S(1)}, u32[]{:S(2)}, u32[]{:S(2)}) collective-permute-start(f32[2,2,64]{2,1,0:T(2,128)S(1)} %fusion.21), channel_id=1, source_target_pairs={{0,1},{1,0},{2,3},{3,2},{4,5},{5,4},{6,7},{7,6},{8,9},{9,8},{10,11... | collective-permute-start | bytes 3080 | tf_op jit(solution)/shard_map/ppermute | solution.py:12
  78.5 3.6 %collective-permute-start.7 = (f32[1,2,64]{2,1,0:T(2,128)S(1)}, f32[1,2,64]{2,1,0:T(2,128)S(1)}, u32[]{:S(2)}, u32[]{:S(2)}) collective-permute-start(f32[1,2,64]{2,1,0:T(2,128)S(1)} %constant_dynamic-slice_fusion), channel_id=1, source_target_pairs={{0,2},{1,3},{2,0},{3,1},{4,6},{5,7},{6,4},{7,5},{8,10},{9,11},{10,... | collective-permute-start | bytes 1544 | tf_op jit(solution)/shard_map/ppermute | solution.py:12
where the time goes:
time: 83.2 us; the launch traced here: 82.8 us
  blocking collectives  29.9 us (36%)
  starting transfers between devices  18.6 us (22%)
  waiting for transfers between devices  18.3 us (22%)
  matrix products  6.38 us (8%)
  local copies, waits for them, and re-layouts  4.8 us (6%)
  other arithmetic  4.49 us (5%)
    psum x1, blocking collectives, on_device(): total = lax.psum(jnp.sum(block * block, axis=1), 'dp')  29.9 us
    ppermute x8, waiting for transfers between devices, partner(): return lax.ppermute(value, axis, pairs)  15.6 us
    all_to_all x1, starting transfers between devices, on_device(): lax.all_to_all(tag_table, 'dp', split_axis=1, concat_axis=0, tiled=True)  7.02 us
    all_to_all x1, starting transfers between devices, on_device(): lax.all_to_all(partials.reshape(LOCAL, devices, width), 'dp', split_axis=...  6.02 us
    ppermute x8, starting transfers between devices, partner(): return lax.ppermute(value, axis, pairs)  5.59 us
    dot_general x1, matrix products, on_device(): lax.dot_general(spread, in_factors, (((0,), (0,)), ((), ())), preferred_e...  4.18 us
    all_to_all x1, waiting for transfers between devices, on_device(): lax.all_to_all(partials.reshape(LOCAL, devices, width), 'dp', split_axis=...  2.76 us
    dot_general x1, matrix products, on_device(): lax.dot_general(gradients, proj_out, contract, preferred_element_type=jnp...  2.07 us
  transfers between devices with their start and end apart: 10, of which 8 were waited for; matrix products, arithmetic and copies ran while one was open for 14% of the time, Pallas kernels for 0%

commit v1 on v0

v1 whole, which is shorter than its diff:
```python
import functools

import jax
import jax.numpy as jnp
from jax import lax
from jax.experimental import pallas as pl
from jax.experimental.pallas import tpu as pltpu
from jax.sharding import PartitionSpec as P

MESH = pl.DeviceIdType.MESH
SLOTS = 4
HEAD = 80
QUARTERS = 4
CHUNK = 2048
NT = (((1,), (1,)), ((), ()))
NN = (((1,), (0,)), ((), ()))


def iota(shape, dim):
    return lax.broadcasted_iota(jnp.int32, shape, dim)


def kernel(
    n, act_ref, grad_ref, pin_ref, pout_ref, tgt_ref, tok_ref, rows_ref, out_ref,
    act, grad, pin, pout, stage, table, ids, ids_next, ids_prev, comb, comb_next, sent, arrived,
    load_sem, gather_send, gather_recv, near_send, near_recv, last_send, last_recv,
):
    me = lax.axis_index("dp")
    tokens = act_ref.shape[0]
    rank = pin_ref.shape[0]
    outer, inner = 4, n // 8
    mid_step, outer_step = 2, n // 4
    core = lax.rem(me, 2)
    mid = lax.rem(me // 2, inner)
    out_at = me // outer_step

    barrier = pltpu.get_barrier_semaphore()

    def greet(k, carry):
        pl.semaphore_signal(
            barrier, inc=1, device_id={"dp": lax.rem(me + k, n)}, device_id_type=MESH
        )
        return carry

    lax.fori_loop(1, n, greet, 0)

    loads = []
    for source, proj, source_v, proj_v in (
        (grad_ref, pout_ref, grad, pout),
        (act_ref, pin_ref, act, pin),
    ):
        group = []
        for start in range(0, source.shape[1], CHUNK):
            at = pl.ds(start, CHUNK)
            for src, dst in ((proj, proj_v), (source, source_v)):
                copy = pltpu.make_async_copy(
                    src.at[:, at], dst.at[:, at], load_sem.at[len(loads)]
                )
                copy.start()
                loads.append(copy)
                group.append((copy, start))
    out_chunks = grad_ref.shape[1] // CHUNK

    width = stage.shape[1]
    per = tgt_ref.shape[0]
    for q in range(QUARTERS):
        stage[q * per:(q + 1) * per, :] = tgt_ref[:, q * width:(q + 1) * width].astype(jnp.float32)
    height = QUARTERS * per

    def block_of(index):
        return table.at[pl.ds(pl.multiple_of(index * height, height), height), :]

    table[pl.ds(pl.multiple_of(me * height, height), height), :] = stage[...].astype(jnp.bfloat16)
    ids[...] = jnp.broadcast_to(tok_ref[...], ids.shape)

    pl.semaphore_wait(barrier, n - 1)

    sends = []

    def push(index, device):
        copy = pltpu.make_async_remote_copy(
            src_ref=block_of(index), dst_ref=block_of(index),
            send_sem=gather_send.at[len(sends)], recv_sem=gather_recv.at[index],
            device_id={"dp": device}, device_id_type=MESH,
        )
        copy.start()
        sends.append(copy)

    def await_block(index):
        pltpu.make_async_copy(block_of(index), block_of(index), gather_recv.at[index]).wait()

    def place(o, m, c):
        return o * outer_step + m * mid_step + c

    def near(src, dst, slot, device):
        return pltpu.make_async_remote_copy(
            src_ref=src, dst_ref=dst, send_sem=near_send.at[slot], recv_sem=near_recv.at[slot],
            device_id={"dp": device}, device_id_type=MESH,
        )

    before, after = lax.rem(me + n - 1, n), lax.rem(me + 1, n)
    to_before = near(ids, ids_next, 0, before)
    to_after = near(ids, ids_prev, 1, after)
    head_to_before = near(comb.at[:HEAD, :], comb_next, 2, before)

    other = [lax.rem(out_at + k, outer) for k in range(1, outer)]
    other_mid = [lax.rem(mid + k, inner) for k in range(1, inner)]
    sibling = me + 1 - 2 * core
    for o in other:
        push(me, place(o, mid, core))
    for m in other_mid:
        push(me, place(out_at, m, core))
    push(me, sibling)
    pl.when(me > 0)(to_before.start)
    pl.when(me < n - 1)(to_after.start)

    def forward_outer():
        for o in other:
            index = place(o, mid, core)
            await_block(index)
            for m in other_mid:
                push(index, place(out_at, m, core))
            push(index, sibling)

    def forward_mid():
        for o in [out_at] + other:
            for m in other_mid:
                index = place(o, m, core)
                await_block(index)
                push(index, sibling)

    def factors(first, count, source_v, proj_v):
        total = jnp.zeros((tokens, rank), jnp.float32)
        for k in range(count):
            loads[first + 2 * k].wait()
            loads[first + 2 * k + 1].wait()
            at = slice(k * CHUNK, (k + 1) * CHUNK)
            total += lax.dot_general(
                source_v[:, at], proj_v[:, at], NT, preferred_element_type=jnp.float32
            )
        return total

    out_factors = factors(0, out_chunks, grad, pout)
    in_factors = factors(2 * out_chunks, act_ref.shape[1] // CHUNK, act, pin)
    comb_own = jnp.concatenate([out_factors, in_factors], axis=1)
    comb[...] = comb_own.astype(jnp.bfloat16)
    pl.when(me > 0)(head_to_before.start)
    forward_outer()

    swap_own = pltpu.roll(comb_own, rank, 1).astype(jnp.bfloat16)
    pairs = rank // 2
    lanes = 2 * rank
    pick_row = iota((pairs * 8, lanes), 0) // 8
    pick_lane = iota((pairs * 8, lanes), 1)
    pick = [
        (pick_lane == 2 * pick_row + parity).astype(jnp.float32).astype(jnp.bfloat16)
        for parity in range(2)
    ]
    first = ids[:, 0:1]
    last = ids[:, tokens - 1:tokens]
    low_lanes = iota((pairs * 8, lanes), 1) < rank

    def sketch_part(values, swapped, token_ids):
        count = values.shape[0]
        mask = (token_ids[:, :count] == first + iota((8, count), 0)).astype(jnp.float32)
        parts = []
        for parity, matched in ((0, swapped), (1, values)):
            spread = lax.dot_general(pick[parity], values, NT, preferred_element_type=jnp.float32)
            spread = spread.reshape(pairs, 8, count) * mask[None]
            spread = spread.reshape(pairs * 8, count).astype(jnp.bfloat16)
            parts.append(lax.dot_general(spread, matched, NN, preferred_element_type=jnp.float32))
        return jnp.where(low_lanes, parts[0], parts[1])

    sketch = sketch_part(comb[...], swap_own, ids[...])
    forward_mid()

    @pl.when(me < n - 1)
    def _():
        to_before.wait_recv()
        head_to_before.wait_recv()

    @pl.when(me == n - 1)
    def _():
        ids_next[...] = jnp.full(ids_next.shape, -1, jnp.int32)
        comb_next[...] = jnp.zeros_like(comb_next)

    @pl.when(me > 0)
    def _():
        to_after.wait_recv()

    @pl.when(me == 0)
    def _():
        ids_prev[...] = jnp.full(ids_prev.shape, -1, jnp.int32)

    values = comb_next[...]
    swapped = pltpu.roll(values.astype(jnp.float32), rank, 1).astype(jnp.bfloat16)
    sketch += sketch_part(values, swapped, ids_next[...])
    tiles = sketch.reshape(pairs, 8, lanes)
    total = jnp.sum(jnp.sum(tiles * tiles, axis=0), axis=1, keepdims=True)
    scale = lax.rsqrt(total / (rank * rank) + 1e-06)
    tiles = tiles * scale[None]
    span = pairs // QUARTERS
    unit = jnp.concatenate(
        [
            jnp.concatenate([tiles[q * span + p] for p in range(span)], axis=1)
            for q in range(QUARTERS)
        ],
        axis=0,
    ).astype(jnp.bfloat16)

    for o in range(outer):
        for m in range(inner):
            await_block(place(o, m, 1 - core))
    every = n * height
    mixed = lax.dot_general(unit, table[...], NT, preferred_element_type=jnp.float32)
    quarter_of = lax.rem(iota((8, every), 1) // per, QUARTERS)
    total = jnp.zeros((8, every), jnp.float32)
    for q in range(QUARTERS):
        total += jnp.where(quarter_of == q, mixed[q * 8:(q + 1) * 8], 0.0)
    high = total.astype(jnp.bfloat16).astype(jnp.float32)
    halves = jnp.concatenate([high, total - high], axis=0).astype(jnp.bfloat16)
    columns = sent.shape[2]
    lane = iota((every, columns), 0)
    fold = (lane // height * per + lax.rem(lane, per) == iota((every, columns), 1))
    fold = fold.astype(jnp.float32).astype(jnp.bfloat16)
    folded = lax.dot_general(halves, fold, NN, preferred_element_type=jnp.float32)
    scores = (folded[:8] + folded[8:]) / rank

    samples = rows_ref.shape[1]
    own_rows = samples // n
    goals = []
    for s in range(SLOTS):
        here = first[0:1] + s
        found = jnp.where(iota((1, samples), 1) == here, rows_ref[...], 0)
        goal = jnp.sum(found, axis=1, keepdims=True)
        valid = here <= last[0:1]
        if s == 0:
            valid = valid & (ids_prev[0:1, tokens - 1:tokens] != here)
        goals.append(jnp.where(valid, goal, -1))
    sublane = iota((8, columns), 0)
    position = jnp.where(sublane < own_rows, sublane, samples)
    offsets = [jnp.broadcast_to(goal, (8, columns)) - position for goal in goals]
    lines = [jnp.broadcast_to(scores[s:s + 1], (8, columns)) for s in range(SLOTS)]

    def tile_for(device):
        tile = jnp.zeros((8, columns), jnp.float32)
        for s in range(SLOTS):
            tile += jnp.where(offsets[s] == device * own_rows, lines[s], 0.0)
        return tile

    def last_copy(device, source):
        return pltpu.make_async_remote_copy(
            src_ref=sent.at[device], dst_ref=arrived.at[me],
            send_sem=last_send.at[device], recv_sem=last_recv.at[source],
            device_id={"dp": device}, device_id_type=MESH,
        )

    def deliver(k, carry):
        device = lax.rem(me + k, n)
        sent[device] = tile_for(device)
        last_copy(device, me).start()
        return carry

    lax.fori_loop(1, n, deliver, 0, unroll=n <= 16)
    arrived[me] = tile_for(me)

    def receive(k, carry):
        source = lax.rem(me + k, n)
        pltpu.make_async_copy(arrived.at[source], arrived.at[source], last_recv.at[source]).wait()
        return carry

    lax.fori_loop(1, n, receive, 0, unroll=n <= 16)
    result = jnp.sum(arrived[...], axis=0)
    out_ref[...] = result[:own_rows, :out_ref.shape[1]]

    def sent_off(k, carry):
        device = lax.rem(me + k, n)
        last_copy(device, me).wait_send()
        return carry

    lax.fori_loop(1, n, sent_off, 0, unroll=n <= 16)
    for copy in sends:
        copy.wait_send()

    @pl.when(me > 0)
    def _():
        to_before.wait_send()
        head_to_before.wait_send()

    @pl.when(me < n - 1)
    def _():
        to_after.wait_send()


def on_device(activations, gradients, proj_in, proj_out, targets, token_samples, sample_rows):
    n = lax.axis_size("dp")
    tokens, d_in = activations.shape
    d_out = gradients.shape[1]
    rank = proj_in.shape[0]
    per, square = targets.shape
    samples = sample_rows.shape[0]
    height = QUARTERS * per
    width = square // QUARTERS
    columns = max(128, n * per)
    gather_sends = 3 + 4 * (n // 8 - 1) + n // 2
    vmem = pl.BlockSpec(memory_space=pltpu.VMEM)
    hbm = pl.BlockSpec(memory_space=pl.ANY)
    bf16, f32 = jnp.bfloat16, jnp.float32
    return pl.pallas_call(
        functools.partial(kernel, n),
        out_shape=jax.ShapeDtypeStruct((samples // n, n * per), f32),
        in_specs=[hbm, hbm, hbm, hbm, vmem, vmem, vmem],
        out_specs=vmem,
        scratch_shapes=[
            pltpu.VMEM((tokens, d_in), bf16),
            pltpu.VMEM((tokens, d_out), bf16),
            pltpu.VMEM((rank, d_in), bf16),
            pltpu.VMEM((rank, d_out), bf16),
            pltpu.VMEM((height, width), f32),
            pltpu.VMEM((n * height, width), bf16),
            pltpu.VMEM((8, tokens), jnp.int32),
            pltpu.VMEM((8, tokens), jnp.int32),
            pltpu.VMEM((8, tokens), jnp.int32),
            pltpu.VMEM((tokens, 2 * rank), bf16),
            pltpu.VMEM((HEAD, 2 * rank), bf16),
            pltpu.VMEM((n, 8, columns), f32),
            pltpu.VMEM((n, 8, columns), f32),
            pltpu.SemaphoreType.DMA((2 * (d_in + d_out) // CHUNK,)),
            pltpu.SemaphoreType.DMA((gather_sends,)),
            pltpu.SemaphoreType.DMA((n,)),
            pltpu.SemaphoreType.DMA((3,)),
            pltpu.SemaphoreType.DMA((3,)),
            pltpu.SemaphoreType.DMA((n,)),
            pltpu.SemaphoreType.DMA((n,)),
        ],
        compiler_params=pltpu.CompilerParams(
            collective_id=0, has_side_effects=True, vmem_limit_bytes=56 * 1024 * 1024
        ),
    )(
        activations, gradients, proj_in, proj_out, targets,
        token_samples.reshape(1, tokens), sample_rows.reshape(1, samples),
    )


def solution(mesh):
    in_specs = (
        P(("groups", "dp"), None),
        P(("groups", "dp"), None),
        P(),
        P(),
        P(("groups", "dp"), None),
        P(("groups", "dp")),
        P("groups"),
    )
    out_specs = P(("groups", "dp"), None)
    return jax.shard_map(
        on_device, mesh=mesh, in_specs=in_specs, out_specs=out_specs, check_vma=False
    )
```

time: 83.2 us -> 23.4 us (0.28)
  blocking collectives: 29.9 us -> 0 us
  Pallas kernels: 0 us -> 21.9 us
  starting transfers between devices: 18.6 us -> 0 us
  waiting for transfers between devices: 18.3 us -> 0 us
  matrix products: 6.38 us -> 0 us
  other arithmetic: 4.49 us -> 0 us
  local copies, waits for them, and re-layouts: 4.8 us -> 1.24 us
    psum x1 -> x0, blocking collectives: 29.9 us -> none  [on_device(): total = lax.psum(jnp.sum(block * block, axis=1), 'dp')]
    pallas_call x0 -> x1, Pallas kernels: none -> 21.9 us  [on_device(): pl.pallas_call(functools.partial(kernel, n), out_shape=jax.ShapeDtypeStru...]
    ppermute x8 -> x0, waiting for transfers between devices: 15.6 us -> none  [partner(): return lax.ppermute(value, axis, pairs)]
    all_to_all x2 -> x0, starting transfers between devices: 13 us -> none  [the longest x1 7.02 us: on_device(): lax.all_to_all(tag_table, 'dp', split_axis=1, concat_axis=0, tiled=True)]
    dot_general x3 -> x0, matrix products: 6.38 us -> none  [the longest x1 4.18 us: on_device(): lax.dot_general(spread, in_factors, (((0,), (0,)), ((), ())), preferred_e...]
    ppermute x8 -> x0, starting transfers between devices: 5.59 us -> none  [partner(): return lax.ppermute(value, axis, pairs)]
    all_to_all x2 -> x0, waiting for transfers between devices: 2.77 us -> none  [the longest x1 2.76 us: on_device(): lax.all_to_all(partials.reshape(LOCAL, devices, width), 'dp', split_axis=...]
    reshape x5 -> x0, local copies, waits for them, and re-layouts: 1.75 us -> none  [the longest x2 0.97 us: on_device(): targets.reshape(target_count, side_count, side_count, sum_count, width)]
  transfers between devices with their start and end apart: 10 -> 0, of which waited for: 8 -> 0; matrix products, arithmetic and copies ran while one was open for 14% -> 0% of each run, Pallas kernels for 0% -> 0%
where the time goes in v1:
time: 23.4 us; the launch traced here: 23.2 us
  Pallas kernels  21.9 us (94%)
  local copies, waits for them, and re-layouts  1.24 us (5%)
    pallas_call x1, Pallas kernels, on_device(): pl.pallas_call(functools.partial(kernel, n), out_shape=jax.ShapeDtypeStru...  21.9 us
    unnamed x1, local copies, waits for them, and re-layouts  1.24 us

profile of v1, /device:TPU:0, one launch (start us, length us, event | category | flops | bytes accessed | tf_op | source)
XLA Modules:
  0.0 23.2 jit_solution(4265887538488287084)
XLA Ops:
  0.0 21.9 %shard_map.73 = f32[2,64]{1,0:T(2,128)} custom-call(bf16[128,14336]{1,0:T(8,128)(2,1)} %act_ref.1, bf16[128,8192]{1,0:T(8,128)(2,1)} %grad_ref.1, bf16[64,14336]{1,0:T(8,128)(2,1)} %pin_ref.1, bf16[64,8192]{1,0:T(8,128)(2,1)} %pout_ref.1, bf16[4,4096]{1,0:T(4,128)(2,1)} %tgt_ref.1, s32[1,128]{1,0:T(1,128)} %bitcast.2, s32[1,32]{1,0:T(1,128)} %bitcast.3), custom_call_target="tpu_custom_call" | custom-call | tf_op jit(solution)/shard_map/pallas_call | solution.py:309
  21.9 1.2 %copy.9 = f32[2,64]{1,0:T(2,128)} copy(f32[2,64]{1,0:T(2,128)} %shard_map.73) | data formatting | bytes 1024

commit v2 on v1

--- a/solution.py
+++ b/solution.py
@@ -12,6 +12,7 @@
 HEAD = 80
 QUARTERS = 4
 CHUNK = 2048
+BEGIN_AT, OUTER_AT = 4, 12
 NT = (((1,), (1,)), ((), ()))
 NN = (((1,), (0,)), ((), ()))
 
@@ -22,8 +23,8 @@
 
 def kernel(
     n, act_ref, grad_ref, pin_ref, pout_ref, tgt_ref, tok_ref, rows_ref, out_ref,
-    act, grad, pin, pout, stage, table, ids, ids_next, ids_prev, comb, comb_next, sent, arrived,
-    load_sem, gather_send, gather_recv, near_send, near_recv, last_send, last_recv,
+    act, grad, pin, pout, stage, table, units, goals_all, ids, ids_next, ids_prev, comb, comb_next, sent, arrived,
+    load_sem, gather_send, gather_recv, near_send, near_recv, mid_send, mid_recv, last_send, last_recv,
 ):
     me = lax.axis_index("dp")
     tokens = act_ref.shape[0]
@@ -60,6 +61,16 @@
                 loads.append(copy)
                 group.append((copy, start))
     out_chunks = grad_ref.shape[1] // CHUNK
+    STEPS = out_chunks + act_ref.shape[1] // CHUNK
+
+    pairs = rank // 2
+    lanes = 2 * rank
+    pick_row = iota((pairs * 8, lanes), 0) >> 3
+    pick_lane = iota((pairs * 8, lanes), 1)
+    pick = [
+        (pick_lane == 2 * pick_row + parity).astype(jnp.float32).astype(jnp.bfloat16)
+        for parity in range(2)
+    ]
 
     width = stage.shape[1]
     per = tgt_ref.shape[0]
@@ -70,10 +81,11 @@
     def block_of(index):
         return table.at[pl.ds(pl.multiple_of(index * height, height), height), :]
 
-    table[pl.ds(pl.multiple_of(me * height, height), height), :] = stage[...].astype(jnp.bfloat16)
+    own_block = 2 * out_at + core
+    table[pl.ds(pl.multiple_of(own_block * height, height), height), :] = stage[...].astype(
+        jnp.bfloat16
+    )
     ids[...] = jnp.broadcast_to(tok_ref[...], ids.shape)
-
-    pl.semaphore_wait(barrier, n - 1)
 
     sends = []
 
@@ -106,32 +118,27 @@
     other = [lax.rem(out_at + k, outer) for k in range(1, outer)]
     other_mid = [lax.rem(mid + k, inner) for k in range(1, inner)]
     sibling = me + 1 - 2 * core
-    for o in other:
-        push(me, place(o, mid, core))
-    for m in other_mid:
-        push(me, place(out_at, m, core))
-    push(me, sibling)
-    pl.when(me > 0)(to_before.start)
-    pl.when(me < n - 1)(to_after.start)
+
+    def begin():
+        pl.semaphore_wait(barrier, n - 1)
+        for o in other:
+            push(own_block, place(o, mid, core))
+        push(own_block, sibling)
+        pl.when(me > 0)(to_before.start)
+        pl.when(me < n - 1)(to_after.start)
 
     def forward_outer():
         for o in other:
-            index = place(o, mid, core)
+            index = 2 * o + core
             await_block(index)
-            for m in other_mid:
-                push(index, place(out_at, m, core))
             push(index, sibling)
 
-    def forward_mid():
-        for o in [out_at] + other:
-            for m in other_mid:
-                index = place(o, m, core)
-                await_block(index)
-                push(index, sibling)
+    steps = {BEGIN_AT: begin, OUTER_AT: forward_outer}
 
     def factors(first, count, source_v, proj_v):
         total = jnp.zeros((tokens, rank), jnp.float32)
         for k in range(count):
+            steps.get(first // 2 + k, lambda: None)()
             loads[first + 2 * k].wait()
             loads[first + 2 * k + 1].wait()
             at = slice(k * CHUNK, (k + 1) * CHUNK)
@@ -144,25 +151,18 @@
     in_factors = factors(2 * out_chunks, act_ref.shape[1] // CHUNK, act, pin)
     comb_own = jnp.concatenate([out_factors, in_factors], axis=1)
     comb[...] = comb_own.astype(jnp.bfloat16)
+    steps.get(STEPS, lambda: None)()
     pl.when(me > 0)(head_to_before.start)
-    forward_outer()
+    steps.get(STEPS + 1, lambda: None)()
 
     swap_own = pltpu.roll(comb_own, rank, 1).astype(jnp.bfloat16)
-    pairs = rank // 2
-    lanes = 2 * rank
-    pick_row = iota((pairs * 8, lanes), 0) // 8
-    pick_lane = iota((pairs * 8, lanes), 1)
-    pick = [
-        (pick_lane == 2 * pick_row + parity).astype(jnp.float32).astype(jnp.bfloat16)
-        for parity in range(2)
-    ]
     first = ids[:, 0:1]
     last = ids[:, tokens - 1:tokens]
     low_lanes = iota((pairs * 8, lanes), 1) < rank
 
     def sketch_part(values, swapped, token_ids):
         count = values.shape[0]
-        mask = (token_ids[:, :count] == first + iota((8, count), 0)).astype(jnp.float32)
+        mask = (token_ids[:, :count] == first + (iota((8, count), 0) & (SLOTS - 1))).astype(jnp.float32)
         parts = []
         for parity, matched in ((0, swapped), (1, values)):
             spread = lax.dot_general(pick[parity], values, NT, preferred_element_type=jnp.float32)
@@ -172,12 +172,11 @@
         return jnp.where(low_lanes, parts[0], parts[1])
 
     sketch = sketch_part(comb[...], swap_own, ids[...])
-    forward_mid()
+    steps.get(STEPS + 2, lambda: None)()
 
     @pl.when(me < n - 1)
     def _():
         to_before.wait_recv()
-        head_to_before.wait_recv()
 
     @pl.when(me == n - 1)
     def _():
@@ -191,6 +190,43 @@
     @pl.when(me == 0)
     def _():
         ids_prev[...] = jnp.full(ids_prev.shape, -1, jnp.int32)
+
+    samples = rows_ref.shape[1]
+    own_rows = samples // n
+    for s in range(SLOTS):
+        here = first[0:1] + s
+        found = jnp.where(iota((1, samples), 1) == here, rows_ref[...], 0)
+        goal = jnp.sum(found, axis=1, keepdims=True)
+        valid = here <= last[0:1]
+        if s == 0:
+            valid = valid & (ids_prev[0:1, tokens - 1:tokens] != here)
+        goals_all[mid, s:s + 1, :] = jnp.broadcast_to(jnp.where(valid, goal, -1), (1, 128))
+
+    def goal_copy(k, m, source):
+        return pltpu.make_async_remote_copy(
+            src_ref=goals_all.at[mid], dst_ref=goals_all.at[mid],
+            send_sem=mid_send.at[0, k], recv_sem=mid_recv.at[0, source],
+            device_id={"dp": place(out_at, m, core)}, device_id_type=MESH,
+        )
+
+    rows_of = SLOTS * QUARTERS
+
+    def unit_rows(m):
+        return units.at[pl.ds(pl.multiple_of(m * rows_of, rows_of), rows_of), :]
+
+    def unit_copy(k, m, source):
+        return pltpu.make_async_remote_copy(
+            src_ref=unit_rows(mid), dst_ref=unit_rows(mid),
+            send_sem=mid_send.at[1, k], recv_sem=mid_recv.at[1, source],
+            device_id={"dp": place(out_at, m, core)}, device_id_type=MESH,
+        )
+
+    for k, m in enumerate(other_mid):
+        goal_copy(k, m, mid).start()
+
+    @pl.when(me < n - 1)
+    def _():
+        head_to_before.wait_recv()
 
     values = comb_next[...]
     swapped = pltpu.roll(values.astype(jnp.float32), rank, 1).astype(jnp.bfloat16)
@@ -200,51 +236,66 @@
     scale = lax.rsqrt(total / (rank * rank) + 1e-06)
     tiles = tiles * scale[None]
     span = pairs // QUARTERS
+    upper = iota((8, lanes), 0) < SLOTS
     unit = jnp.concatenate(
         [
-            jnp.concatenate([tiles[q * span + p] for p in range(span)], axis=1)
-            for q in range(QUARTERS)
+            jnp.concatenate(
+                [
+                    jnp.where(upper, tiles[q * span + p], tiles[(q + 1) * span + p])
+                    for p in range(span)
+                ],
+                axis=1,
+            )
+            for q in range(0, QUARTERS, 2)
         ],
         axis=0,
     ).astype(jnp.bfloat16)
-
+    units[pl.ds(pl.multiple_of(mid * rows_of, rows_of), rows_of), :] = unit
+    for k, m in enumerate(other_mid):
+        unit_copy(k, m, mid).start()
+
+    every = 2 * outer * height
+    columns = sent.shape[2]
+    lane = iota((every, columns), 0)
+    device_of = lax.rem(lane // height, 2) + lane // (2 * height) * outer_step + mid * mid_step
+    fold = device_of * per + lax.rem(lane, per) == iota((every, columns), 1)
+    fold = fold.astype(jnp.float32).astype(jnp.bfloat16)
     for o in range(outer):
-        for m in range(inner):
-            await_block(place(o, m, 1 - core))
-    every = n * height
-    mixed = lax.dot_general(unit, table[...], NT, preferred_element_type=jnp.float32)
-    quarter_of = lax.rem(iota((8, every), 1) // per, QUARTERS)
-    total = jnp.zeros((8, every), jnp.float32)
-    for q in range(QUARTERS):
-        total += jnp.where(quarter_of == q, mixed[q * 8:(q + 1) * 8], 0.0)
+        await_block(2 * o + 1 - core)
+    for k, m in enumerate(other_mid):
+        goal_copy(k, m, m).wait_recv()
+        pltpu.make_async_copy(unit_rows(m), unit_rows(m), mid_recv.at[1, m]).wait()
+    mixed = lax.dot_general(units[...], table[...], NT, preferred_element_type=jnp.float32)
+    quarter_row = lax.rem(iota((rows_of, every), 0) // SLOTS, QUARTERS)
+    quarter_lane = lax.rem(iota((rows_of, every), 1) // per, QUARTERS)
+    same = quarter_row == quarter_lane
+    summed = []
+    for m in range(inner):
+        part = jnp.where(same, mixed[m * rows_of:(m + 1) * rows_of], 0.0)
+        part = part[:8] + part[8:]
+        summed.append(part + pltpu.roll(part, SLOTS, 0))
+    first_half = iota((8, every), 0) < SLOTS
+    total = jnp.concatenate(
+        [jnp.where(first_half, summed[m], summed[m + 1]) for m in range(0, inner, 2)], axis=0
+    )
+    slots = inner * SLOTS
     high = total.astype(jnp.bfloat16).astype(jnp.float32)
     halves = jnp.concatenate([high, total - high], axis=0).astype(jnp.bfloat16)
-    columns = sent.shape[2]
-    lane = iota((every, columns), 0)
-    fold = (lane // height * per + lax.rem(lane, per) == iota((every, columns), 1))
-    fold = fold.astype(jnp.float32).astype(jnp.bfloat16)
     folded = lax.dot_general(halves, fold, NN, preferred_element_type=jnp.float32)
-    scores = (folded[:8] + folded[8:]) / rank
-
-    samples = rows_ref.shape[1]
-    own_rows = samples // n
-    goals = []
-    for s in range(SLOTS):
-        here = first[0:1] + s
-        found = jnp.where(iota((1, samples), 1) == here, rows_ref[...], 0)
-        goal = jnp.sum(found, axis=1, keepdims=True)
-        valid = here <= last[0:1]
-        if s == 0:
-            valid = valid & (ids_prev[0:1, tokens - 1:tokens] != here)
-        goals.append(jnp.where(valid, goal, -1))
+    scores = (folded[:slots] + folded[slots:]) / rank
+
     sublane = iota((8, columns), 0)
     position = jnp.where(sublane < own_rows, sublane, samples)
-    offsets = [jnp.broadcast_to(goal, (8, columns)) - position for goal in goals]
-    lines = [jnp.broadcast_to(scores[s:s + 1], (8, columns)) for s in range(SLOTS)]
+    offsets = [
+        jnp.broadcast_to(goals_all[m, s:s + 1, 0:1], (8, columns)) - position
+        for m in range(inner)
+        for s in range(SLOTS)
+    ]
+    lines = [jnp.broadcast_to(scores[s:s + 1], (8, columns)) for s in range(slots)]
 
     def tile_for(device):
         tile = jnp.zeros((8, columns), jnp.float32)
-        for s in range(SLOTS):
+        for s in range(slots):
             tile += jnp.where(offsets[s] == device * own_rows, lines[s], 0.0)
         return tile
 
@@ -281,6 +332,9 @@
     lax.fori_loop(1, n, sent_off, 0, unroll=n <= 16)
     for copy in sends:
         copy.wait_send()
+    for k, m in enumerate(other_mid):
+        goal_copy(k, m, mid).wait_send()
+        unit_copy(k, m, mid).wait_send()
 
     @pl.when(me > 0)
     def _():
@@ -302,7 +356,8 @@
     height = QUARTERS * per
     width = square // QUARTERS
     columns = max(128, n * per)
-    gather_sends = 3 + 4 * (n // 8 - 1) + n // 2
+    inner = n // 8
+    blocks = n // inner
     vmem = pl.BlockSpec(memory_space=pltpu.VMEM)
     hbm = pl.BlockSpec(memory_space=pl.ANY)
     bf16, f32 = jnp.bfloat16, jnp.float32
@@ -317,7 +372,9 @@
             pltpu.VMEM((rank, d_in), bf16),
             pltpu.VMEM((rank, d_out), bf16),
             pltpu.VMEM((height, width), f32),
-            pltpu.VMEM((n * height, width), bf16),
+            pltpu.VMEM((blocks * height, width), bf16),
+            pltpu.VMEM((inner * SLOTS * QUARTERS, width), bf16),
+            pltpu.VMEM((inner, 8, 128), jnp.int32),
             pltpu.VMEM((8, tokens), jnp.int32),
             pltpu.VMEM((8, tokens), jnp.int32),
             pltpu.VMEM((8, tokens), jnp.int32),
@@ -326,10 +383,12 @@
             pltpu.VMEM((n, 8, columns), f32),
             pltpu.VMEM((n, 8, columns), f32),
             pltpu.SemaphoreType.DMA((2 * (d_in + d_out) // CHUNK,)),
-            pltpu.SemaphoreType.DMA((gather_sends,)),
-            pltpu.SemaphoreType.DMA((n,)),
+            pltpu.SemaphoreType.DMA((blocks - 1,)),
+            pltpu.SemaphoreType.DMA((blocks,)),
             pltpu.SemaphoreType.DMA((3,)),
             pltpu.SemaphoreType.DMA((3,)),
+            pltpu.SemaphoreType.DMA((2, inner)),
+            pltpu.SemaphoreType.DMA((2, inner)),
             pltpu.SemaphoreType.DMA((n,)),
             pltpu.SemaphoreType.DMA((n,)),
         ],

time: 23.4 us -> 23.1 us (0.987)
    pallas_call x1, Pallas kernels: 21.9 us -> 21.7 us  [on_device(): pl.pallas_call(functools.partial(kernel, n), out_shape=jax.ShapeDtypeStru...]
where the time goes in v2:
time: 23.1 us; the launch traced here: 22.9 us
  Pallas kernels  21.7 us (94%)
  local copies, waits for them, and re-layouts  1.24 us (5%)
    pallas_call x1, Pallas kernels, on_device(): pl.pallas_call(functools.partial(kernel, n), out_shape=jax.ShapeDtypeStru...  21.7 us
    unnamed x1, local copies, waits for them, and re-layouts  1.24 us

profile of v2, /device:TPU:0, one launch (start us, length us, event | category | flops | bytes accessed | tf_op | source)
XLA Modules:
  0.0 22.9 jit_solution(674082549138461363)
XLA Ops:
  0.0 21.7 %shard_map.73 = f32[2,64]{1,0:T(2,128)} custom-call(bf16[128,14336]{1,0:T(8,128)(2,1)} %act_ref.1, bf16[128,8192]{1,0:T(8,128)(2,1)} %grad_ref.1, bf16[64,14336]{1,0:T(8,128)(2,1)} %pin_ref.1, bf16[64,8192]{1,0:T(8,128)(2,1)} %pout_ref.1, bf16[4,4096]{1,0:T(4,128)(2,1)} %tgt_ref.1, s32[1,128]{1,0:T(1,128)} %bitcast.2, s32[1,32]{1,0:T(1,128)} %bitcast.3), custom_call_target="tpu_custom_call" | custom-call | tf_op jit(solution)/shard_map/pallas_call | solution.py:364
  21.7 1.2 %copy.9 = f32[2,64]{1,0:T(2,128)} copy(f32[2,64]{1,0:T(2,128)} %shard_map.73) | data formatting | bytes 1024
